TPU v7x, 768 devices: a whole 4x8x12 slice. The times are simulated.
768 devices in a mesh: grp: 32 (over x, y), shard: 24 (over z, core).
Axes of the slice: x: 4, y: 8, z: 12, core: 2. Of those that a mesh axis runs over, the one named last changes fastest.
Arguments:
- table: float32 [393216, 128], P(('grp', 'shard')), may hold values from -6 to 6
- hot_offsets: int32 [12288], P(('grp', 'shard')), may hold values from 0 to 511, as said below
- cold_dest: int32 [6144], P(('grp', 'shard')), may hold values from 0 to 23, as said below
- bag_ids: int32 [24576, 16], P(('grp', 'shard')), may hold values from 0 to 24575, as said below
- bag_len: int32 [24576], P(('grp', 'shard')), may hold values from 1 to 16, as said below
Outputs:
- new_table: float32 [393216, 128], P(('grp', 'shard'))
- pooled: float32 [24576, 128], P(('grp', 'shard'))
Inputs may be any that keep to these rules, and one draw needn't show every extreme that they name: `hot_offsets`: the 16 entries of one device are distinct offsets into that device's own 512 rows. `cold_dest`: entries of device (g, s) are that device's 8 blocks in order. Every device sends exactly 2 blocks to each of 4 devices of its group and none to the others, and every device receives exactly 8 blocks. `bag_ids`: ids below 12288 name hot rows; the others are 12288 plus a row of the sample's own group. Call hot id h's shard index (h // 16) % 24 and cold id i's shard index (i - 12288) // 512. Of the 512 slots of one device, live or not, at most 27 have ids of any one shard index, and in every device exactly 27 have ids of one shard index. `bag_len`: the first sample of each device has 16 live slots.
All inputs are finite; a program needn't handle non-finite values.
Results may differ from a plain program's by a relative error of at most 0.0003.
Values sent between devices are 32-bit elements; how exact they have to be, the bound alone decides.
A program may use at most 32 MiB of HBM per device.

v0:
```python
import math

import jax
import jax.numpy as jnp
from jax import lax
from jax.sharding import PartitionSpec as P


def local(table, hot_offsets, cold_dest, bag_ids, bag_len):
    n_shard = lax.axis_size("shard")
    n_group = lax.axis_size("grp")
    here = lax.axis_index("shard")
    rows_dev, width = table.shape
    hot_dev = hot_offsets.shape[0]
    nblocks = cold_dest.shape[0]
    blk_rows = rows_dev // nblocks
    capacity = max(2, -(-nblocks // n_shard))
    samp_dev, slots = bag_ids.shape
    hot_total = hot_dev * n_group * n_shard
    hot_local = jnp.take(table, hot_offsets, axis=0)
    hot_rows = lax.all_gather(hot_local, "grp", axis=0, tiled=True)
    live = jnp.arange(slots, dtype=jnp.int32)[None, :] < bag_len[:, None]
    masked = jnp.where(live, bag_ids, -1)
    group_ids, group_dest = (
        lax.all_gather(masked, "shard", axis=0, tiled=True),
        lax.all_gather(cold_dest, "shard", axis=0, tiled=True),
    )
    group_dest = group_dest.reshape(n_shard, nblocks)
    block_index = jnp.arange(nblocks, dtype=jnp.int32)
    earlier = block_index[:, None] < block_index[None, :]
    same_own = cold_dest[:, None] == cold_dest[None, :]
    own_rank = jnp.sum((same_own & earlier).astype(jnp.int32), axis=0)
    targets = jnp.arange(n_shard, dtype=jnp.int32)[:, None, None]
    slot_ids = jnp.arange(capacity, dtype=jnp.int32)[None, :, None]
    matches = (cold_dest[None, None, :] == targets) & (own_rank[None, None, :] == slot_ids)
    source_block = jnp.sum(matches.astype(jnp.int32) * block_index[None, None, :], axis=2)
    filled = jnp.any(matches, axis=2)
    blocks = table.reshape(nblocks, blk_rows * width)
    outgoing = jnp.where(filled[:, :, None], blocks[source_block], 0.0)
    received = lax.all_to_all(outgoing, "shard", split_axis=0, concat_axis=0, tiled=True)
    sender_live = jnp.any(group_dest == here, axis=1)
    position = jnp.cumsum(sender_live.astype(jnp.int32)) - 1
    shard_ids = jnp.arange(n_shard, dtype=jnp.int32)
    turns = jnp.arange(nblocks // capacity, dtype=jnp.int32)
    sender_of = jnp.sum(
        ((position[None, :] == turns[:, None]) & sender_live[None, :]).astype(jnp.int32)
        * shard_ids[None, :],
        axis=1,
    )
    sender = sender_of[block_index // capacity]
    slot = block_index % capacity
    new_blocks = received.reshape(n_shard * capacity, blk_rows * width)[sender * capacity + slot]
    new_table = new_blocks.reshape(rows_dev, width)
    same_group = group_dest[:, :, None] == group_dest[:, None, :]
    group_rank = jnp.sum((same_group & earlier[None, :, :]).astype(jnp.int32), axis=1)
    slot_all = jnp.arange(capacity, dtype=jnp.int32)[None, :, None]
    picks = (group_dest[:, None, :] == here) & (group_rank[:, None, :] == slot_all)
    local_block = jnp.sum(picks.astype(jnp.int32) * block_index[None, None, :], axis=2)
    moved_block = sender * nblocks + local_block[sender, slot]
    hot_cols = n_group * hot_dev
    total_cols = hot_cols + rows_dev
    inverse_pos = jnp.full((n_shard * nblocks,), -1, jnp.int32).at[moved_block].set(block_index)
    columns = jnp.concatenate([hot_rows, new_table], axis=0)
    count = lax.axis_size("shard") * samp_dev
    step_rows = math.gcd(count, 512)
    is_hot = (group_ids >= 0) & (group_ids < hot_total)
    hot_mine = is_hot & (group_ids // hot_dev % n_shard == here)
    hot_col = group_ids // hot_dev // n_shard * hot_dev + group_ids % hot_dev
    cold_off = jnp.where(group_ids >= hot_total, group_ids - hot_total, -1)
    group_block = jnp.clip(cold_off // blk_rows, 0, n_shard * nblocks - 1)
    local_pos = inverse_pos[group_block]
    valid = (cold_off >= 0) & (local_pos >= 0)
    cold_col = jnp.where(valid, hot_cols + local_pos * blk_rows + cold_off % blk_rows, total_cols)
    col_blocks = jnp.where(
        hot_mine, hot_col, jnp.where(group_ids >= hot_total, cold_col, total_cols)
    ).reshape(count // step_rows, step_rows, slots)
    row_index = jnp.broadcast_to(
        jnp.arange(step_rows, dtype=jnp.int32)[:, None], (step_rows, slots)
    )

    def pool_block(col_block):
        counts = (
            jnp.zeros((step_rows, total_cols), jnp.float32)
            .at[row_index, col_block]
            .add(1.0, mode="drop")
        )
        return jnp.dot(
            counts, columns, precision=lax.Precision.HIGHEST, preferred_element_type=jnp.float32
        )

    summed = lax.psum_scatter(
        lax.map(pool_block, col_blocks).reshape(count, width),
        "shard",
        scatter_dimension=0,
        tiled=True,
    )
    pooled = summed / bag_len.astype(jnp.float32)[:, None]
    return (new_table, pooled)


def solution(mesh):
    return jax.shard_map(
        local,
        mesh=mesh,
        in_specs=(
            P(("grp", "shard"), None),
            P(("grp", "shard")),
            P(("grp", "shard")),
            P(("grp", "shard"), None),
            P(("grp", "shard")),
        ),
        out_specs=(P(("grp", "shard"), None), P(("grp", "shard"), None)),
        check_vma=False,
    )
```

profile of v0, /device:TPU:1, one launch (start us, length us, event | category | flops | bytes accessed | tf_op | source)
XLA Modules:
  0.0 431.1 jit_solution(15187639856972908564)
XLA Ops:
  7.2 0.7 iota_compare_fusion.3
  7.9 0.8 convert_reduce_fusion.1
  9.1 1.0 reshape.313
  10.1 1.1 gather_fusion
  11.2 0.9 reshape.325
  12.1 0.1 copy.38
  12.2 2.0 broadcast_select_fusion.1
  14.3 16.8 %all-to-all-start = ((f32[24,2,8192]{2,1,0:T(2,128)}), f32[24,2,8192]{2,1,0:T(2,128)S(1)}, u32[]{:S(2)}, u32[]{:S(2)}) async-start(f32[24,2,8192]{2,1,0:T(2,128)} %broadcast_select_fusion.1), calls=%async_computation | async-start | bytes 3145728 | tf_op jit(solution)/shard_map/all_to_all | solution.py:40
  31.2 1.3 dynamic-slice
  33.1 0.2 dynamic-update-slice
  33.4 77.9 %all-reduce = s32[192]{0:T(256)S(1)} all-reduce(s32[192]{0:T(256)S(1)} %dynamic-update-slice), channel_id=1, replica_groups=mesh['grp'=32,'shard'=24] {'shard'}, use_global_device_ids=true, to_apply=%add | all-reduce | flops 192 | bytes 1536
  111.4 0.1 fusion.33
  111.8 24.9 %all-gather = s32[24,32,16]{1,2,0:T(8,128)S(1)} all-gather(s32[1,32,16]{1,2,0:T(8,128)S(1)} %select_bitcast_fusion), channel_id=1, replica_groups=mesh['grp'=32,'shard'=24] {'shard'}, dimensions={0}, use_global_device_ids=true | all-gather | bytes 51200 | tf_op jit(solution)/shard_map/all_gather | solution.py:25
  136.8 0.1 reshape.398
  137.0 0.2 copy.45
  137.1 0.2 reshape.356
  137.3 0.1 add_reduce_fusion
  137.4 0.1 select_reduce_fusion.1
  137.6 0.6 gather_fusion.1
  138.4 0.7 gather_fusion.3
  139.0 0.6 scatter_custom_fusion.1
  139.7 76.2 %gather_fusion.4 = s32[12288]{0:T(1024)S(1)} fusion(s32[192]{0:T(256)S(1)} %scatter_custom_fusion.1, s32[12288]{0:T(1024)S(1)} %broadcast_clamp_fusion), kind=kCustom, calls=%fused_computation.4 | custom fusion | bytes 147456 | tf_op jit(solution)/shard_map/gather | solution.py:71
  215.9 0.2 reshape.393
  216.0 0.1 copy.47
  216.2 0.2 reshape.389
  216.4 0.1 copy.46
  216.5 0.1 fusion.8
  216.7 1.5 gather_fusion.5
  218.3 38.0 %all_gather.11 = f32[512,128]{1,0:T(8,128)S(1)} all-gather(f32[16,128]{1,0:T(8,128)S(1)} %broadcast_select_fusion.2), channel_id=1, replica_groups=mesh['grp'=32,'shard'=24] {'grp'}, dimensions={0}, use_global_device_ids=true | all-gather | bytes 270336 | tf_op jit(solution)/shard_map/all_gather | solution.py:21
  256.4 1.1 reshape.314
  257.5 0.6 gather_fusion.2
  258.3 0.6 copy-done
  258.9 73.2 %while.11 = (s32[]{:T(128)}, f32[3,256,128]{2,1,0:T(8,128)}, s32[3,256,16]{1,0,2:T(4,128)S(1)}, f32[1024,128]{1,0:T(8,128)S(1)}, s32[]{:T(128)}, /*index=5*/s32[2]{0:T(128)S(1)}, s32[2]{0:T(128)S(1)}, f32[]{:T(128)}, f32[]{:T(128)}) while((s32[]{:T(128)}, f32[3,256,128]{2,1,0:T(8,128)}, s32[3,256,16]{1,0,2:T(4,128)S(1)}, ...), condition=%wide.region_11.12_spmd.clone, body=%wide.region_9.11_spmd.clone.sunk | while | flops 402731008 | bytes 5137017 | solution.py:92
  259.1 0.1 copy.56
  259.3 22.2 %scatter_custom_fusion.8 = f32[262144]{0:T(1024)S(1)} fusion(s32[4096]{0:T(1024)S(1)} %reshape.417, f32[4096]{0:T(1024)S(1)} %broadcast.480, f32[]{:T(128)} %constant.135.clone.2..sunk), kind=kCustom, calls=%fused_computation.11.clone.1 | custom fusion | flops 4096 | bytes 1048580 | tf_op jit(solution)/shard_map/while
  281.5 0.2 reshape.418
  281.7 1.6 fusion.43
  283.5 0.1 copy.56
  283.6 0.1 reshape.417
  283.7 22.2 %scatter_custom_fusion.8 = f32[262144]{0:T(1024)S(1)} fusion(s32[4096]{0:T(1024)S(1)} %reshape.417, f32[4096]{0:T(1024)S(1)} %broadcast.480, f32[]{:T(128)} %constant.135.clone.2..sunk), kind=kCustom, calls=%fused_computation.11.clone.1 | custom fusion | flops 4096 | bytes 1048580 | tf_op jit(solution)/shard_map/while
  305.9 0.2 reshape.418
  306.1 1.7 fusion.43
  307.9 0.1 copy.56
  308.2 22.2 %scatter_custom_fusion.8 = f32[262144]{0:T(1024)S(1)} fusion(s32[4096]{0:T(1024)S(1)} %reshape.417, f32[4096]{0:T(1024)S(1)} %broadcast.480, f32[]{:T(128)} %constant.135.clone.2..sunk), kind=kCustom, calls=%fused_computation.11.clone.1 | custom fusion | flops 4096 | bytes 1048580 | tf_op jit(solution)/shard_map/while
  330.3 0.2 reshape.418
  330.5 1.6 fusion.43
  332.2 90.7 %reduce-scatter.2.cloned.1.call-done = f32[32,128]{1,0:T(8,128)} async-done(((f32[768,128]{1,0:T(8,128)}), f32[32,128]{1,0:T(8,128)}) %reduce-scatter.2.cloned.1.call-update) | async-done | bytes 16400 | tf_op jit(solution)/shard_map/reduce_scatter | solution.py:91
  422.9 1.4 broadcast_divide_fusion
  (77 shorter events, 2.1 us)
Async XLA Ops:
  14.3 18.8 %copy-start.5 = (s32[8]{0:T(128)S(1)}, s32[8]{0:T(128)}, u32[]{:S(2)}) copy-start(s32[8]{0:T(128)} %param.9) | copy-start | bytes 100
  14.3 97.5 %copy-start.3 = (s32[32,16]{0,1:T(8,128)S(1)}, s32[32,16]{0,1:T(8,128)}, u32[]{:S(2)}) copy-start(s32[32,16]{0,1:T(8,128)} %param.10) | copy-start | bytes 6148
  14.3 97.5 %copy-start.4 = (s32[32]{0:T(128)S(1)}, s32[32]{0:T(128)}, u32[]{:S(2)}) copy-start(s32[32]{0:T(128)} %param.11) | copy-start | bytes 388
  14.3 242.1 %all-to-all-start = ((f32[24,2,8192]{2,1,0:T(2,128)}), f32[24,2,8192]{2,1,0:T(2,128)S(1)}, u32[]{:S(2)}, u32[]{:S(2)}) async-start(f32[24,2,8192]{2,1,0:T(2,128)} %broadcast_select_fusion.1), calls=%async_computation | async-start | bytes 3145728 | tf_op jit(solution)/shard_map/all_to_all | solution.py:40
  31.1 391.7 %reduce-scatter.2.cloned.1.call-start = ((), (), s32[]{:S(2)}) async-start(), calls=%async_computation.2 | async-start | bytes 409600 | tf_op jit(solution)/shard_map/reduce_scatter | solution.py:91
  139.7 77.1 %copy-start.6 = (s32[16]{0:T(128)S(1)}, s32[16]{0:T(128)}, u32[]{:S(2)}) copy-start(s32[16]{0:T(128)} %param.8) | copy-start | bytes 196
  257.5 0.8 copy-start.1
  257.5 0.8 copy-start.2
  258.2 0.7 copy-start
Sparse Core Ops, SparseCore 0:
  332.3 90.5 reduce-scatter.1
where the time goes:
time: 433 us; the launch traced here: 431 us
  blocking collectives  141 us (33%)
  waiting for transfers between devices  90.7 us (21%)
  local copies, waits for them, and re-layouts  89.5 us (21%)
  other arithmetic  73.1 us (17%)
  starting transfers between devices  16.9 us (4%)
  between operations  15 us (3%)
  matrix products  4.94 us (1%)
    reduce_scatter x1, waiting for transfers between devices, local(): lax.psum_scatter(lax.map(pool_block, col_blocks).reshape(count, width), '...  90.7 us
    unnamed x1, blocking collectives  77.9 us
    gather x1, local copies, waits for them, and re-layouts, local(): local_pos = inverse_pos[group_block]  76.2 us
    while x12, other arithmetic  67 us
    all_gather x1, blocking collectives, local(): hot_rows = lax.all_gather(hot_local, 'grp', axis=0, tiled=True)  38 us
    all_gather x1, blocking collectives, local(): lax.all_gather(masked, 'shard', axis=0, tiled=True)  24.9 us
    all_to_all x1, starting transfers between devices, local(): lax.all_to_all(outgoing, 'shard', split_axis=0, concat_axis=0, tiled=True)  16.8 us
  transfers between devices with their start and end apart: 2, of which 1 were waited for; matrix products, arithmetic and copies ran while one was open for 19% of the time, Pallas kernels for 0%

commit v1 on v0

v1 whole, which is shorter than its diff:
```python
import functools

import jax
import jax.numpy as jnp
from jax import lax
from jax.experimental import pallas as pl
from jax.experimental.pallas import tpu as pltpu
from jax.sharding import PartitionSpec as P

MESH = pl.DeviceIdType.MESH
F32 = jnp.float32
BF16 = jnp.bfloat16
I32 = jnp.int32

NS = 24
NZ = 12
NB = 8
BLK = 64
W = 128
NBLK = NS * NB
SAMP = 32
BAG = 16
SLOTS = SAMP * BAG
HOTD = 16
ROWS = NB * BLK
GROUPS = NS // 4


def iota(shape, axis):
    return lax.broadcasted_iota(I32, shape, axis)


def onehot(mask):
    return jnp.where(mask, 1.0, 0.0).astype(BF16)


def nt(a, b):
    return lax.dot_general(a, b, (((1,), (1,)), ((), ())), preferred_element_type=F32)


def nn(a, b):
    return jnp.dot(a, b, preferred_element_type=F32)


def split2(x):
    hi = x.astype(BF16)
    return hi, (x - hi.astype(F32)).astype(BF16)


def first_row(m):
    return 8 * (m // 3) + 3 * lax.rem(m, 3)


def order(s):
    return lax.rem(s, 2) * NZ + s // 2


def wait_bytes(ref, sem):
    pltpu.make_async_copy(ref, ref, sem).wait()


def kernel(
    ng,
    table_h, off_h, dest_h, ids_h, len_h,
    moved, pooled,
    tbl, ids, off_s, dest_s, len_s,
    abuf, hl, hotloc, hotbuf, msg, req, xbuf, ybuf, cmat, pbuf, sbuf, pin, colv, keyv,
    load_sem, req_send, req_recv, hot_send, hot_recv, one_send, one_recv, two_send, two_recv,
    sib_send, sib_recv, sum_send, sum_recv,
):
    hotc = ng * HOTD
    cols = hotc + ROWS
    me = lax.axis_index("shard")
    grp = lax.axis_index("grp")
    core = lax.rem(me, 2)
    chip = me // 2
    sib = me + 1 - 2 * core
    mine = order(me)
    lane0 = lax.rem(mine, 4)
    three = lax.rem(me, 3) < 2

    loads = [
        pltpu.make_async_copy(table_h, tbl, load_sem.at[0]),
        pltpu.make_async_copy(ids_h, ids, load_sem.at[1]),
        pltpu.make_async_copy(len_h, len_s, load_sem.at[2]),
        pltpu.make_async_copy(off_h, off_s, load_sem.at[3]),
        pltpu.make_async_copy(dest_h, dest_s, load_sem.at[4]),
    ]
    for load in loads:
        load.start()

    barrier = pltpu.get_barrier_semaphore()

    @pl.loop(1, NS)
    def _(k):
        pl.semaphore_signal(
            barrier, inc=1, device_id={"shard": lax.rem(me + k, NS)}, device_id_type=MESH
        )

    @pl.loop(1, ng)
    def _(k):
        pl.semaphore_signal(
            barrier, inc=1, device_id={"grp": lax.rem(grp + k, ng)}, device_id_type=MESH
        )

    for load in loads[1:]:
        load.wait()

    lens = jnp.zeros((SAMP, W), I32)
    row = iota((SAMP, W), 0)
    for n in range(SAMP):
        lens = jnp.where(row == n, len_s[n], lens)
    bag = ids[...]
    hot_total = hotc * NS
    is_hot = bag < hot_total
    owner = bag >> 4
    turn = (owner * 43691) >> 20
    cold = jnp.maximum(bag - hot_total, 0)
    shard = jnp.where(is_hot, owner - turn * NS, cold >> 9)
    col = jnp.where(is_hot, turn * HOTD + (bag & (HOTD - 1)), hotc + (cold & (ROWS - 1)))
    live = iota((SAMP, BAG), 1) < lens[:, :BAG]
    shard = jnp.where(live, shard, 31)
    fields = jnp.concatenate([shard, col >> 5, col & 31], axis=0).astype(F32).astype(BF16)
    spread = nn(fields, onehot(iota((BAG, SLOTS), 0) == (iota((BAG, SLOTS), 1) & (BAG - 1))))
    own = iota((SAMP, SLOTS), 0) == (iota((SAMP, SLOTS), 1) >> 4)
    flat = [
        jnp.sum(jnp.where(own, spread[SAMP * i : SAMP * (i + 1)], 0.0), axis=0, keepdims=True)
        for i in range(3)
    ]
    to = jnp.where(flat[0] == iota((32, SLOTS), 0).astype(F32), 1.0, 0.0)
    to = jnp.where(iota((32, SLOTS), 0) < NS, to, 0.0)
    before = onehot(iota((SLOTS, SLOTS), 0) < iota((SLOTS, SLOTS), 1))
    rank = jnp.sum(to * nn(to.astype(BF16), before), axis=0, keepdims=True)
    place = onehot(
        rank.astype(I32) + 32 * lane0 == iota((W, SLOTS), 0)
    )
    sample1 = ((iota((1, SLOTS), 1) >> 4) + 1).astype(F32)
    packed = jnp.concatenate([to * flat[1], to * flat[2], to * sample1], axis=0).astype(BF16)
    placed = nt(packed, place)
    colpart = 32.0 * placed[0:NS] + placed[32 : 32 + NS]
    samppart = pltpu.roll(placed[64 : 64 + NS], 32, 1)
    dests = jnp.zeros((1, W), I32)
    lane = iota((1, W), 1)
    dlane = 32 * lax.rem(mine + 2, 4)
    for j in range(NB):
        dests = jnp.where(lane == dlane + j, dest_s[j], dests)
    msg[:, 0, :] = colpart + samppart + dests.astype(F32)

    loads[0].wait()
    hi, lo = split2(tbl[...])
    hl[hotc:cols, 0:W] = hi
    hl[hotc:cols, W : 2 * W] = lo
    offs = jnp.zeros((HOTD, ROWS), I32)
    hrow = iota((HOTD, ROWS), 0)
    for k in range(HOTD):
        offs = jnp.where(hrow == k, off_s[k], offs)
    picked = nn(onehot(offs == iota((HOTD, ROWS), 1)), hl[hotc:cols, :])
    hotloc[...] = picked[:, :W] + picked[:, W:]
    for r in range(BLK):
        abuf[r] = tbl[pl.ds(r, NB, stride=BLK), :]

    pl.semaphore_wait(barrier, NS - 1 + ng - 1)

    pltpu.make_async_copy(msg.at[pl.ds(me, 1)], req.at[pl.ds(mine, 1)], req_recv).start()

    @pl.loop(1, NS)
    def _(k):
        peer = lax.rem(me + k, NS)
        pltpu.make_async_remote_copy(
            src_ref=msg.at[pl.ds(peer, 1)], dst_ref=req.at[pl.ds(mine, 1)],
            send_sem=req_send, recv_sem=req_recv,
            device_id={"shard": peer}, device_id_type=MESH,
        ).start()

    hot_here = hotbuf.at[pl.ds(pl.multiple_of(grp * HOTD, HOTD), HOTD)]
    pltpu.make_async_copy(hotloc, hot_here, hot_recv).start()

    @pl.loop(1, ng)
    def _(k):
        pltpu.make_async_remote_copy(
            src_ref=hotloc, dst_ref=hot_here, send_sem=hot_send, recv_sem=hot_recv,
            device_id={"grp": lax.rem(grp + k, ng)}, device_id_type=MESH,
        ).start()

    def relay(peer, count, remote):
        src = abuf.at[pl.ds(first_row(peer), count)]
        dst = xbuf.at[0:count, pl.ds(pl.multiple_of(me * NB, NB), NB), :]
        if remote:
            pltpu.make_async_remote_copy(
                src_ref=src, dst_ref=dst, send_sem=one_send, recv_sem=one_recv,
                device_id={"shard": peer}, device_id_type=MESH,
            ).start()
        else:
            pltpu.make_async_copy(src, dst, one_recv).start()

    def by_count(peer, act):
        @pl.when(lax.rem(peer, 3) < 2)
        def _():
            act(3)

        @pl.when(lax.rem(peer, 3) == 2)
        def _():
            act(2)

    by_count(me, lambda count: relay(me, count, False))

    @pl.loop(1, NS)
    def _(k):
        peer = lax.rem(me + k, NS)
        by_count(peer, lambda count: relay(peer, count, True))

    wait_bytes(req, req_recv)
    asked = req[:, 0, :]
    who = iota((NS, W), 0)
    spot = (iota((NS, W), 1) >> 5) & 3
    first = jnp.where(spot == (who & 3), asked, 0.0)
    second = pltpu.roll(jnp.where(spot == ((who + 1) & 3), asked, 0.0), W - 32, 1)
    pad = jnp.zeros((8 - GROUPS, W), F32)
    gather4 = lambda x: jnp.concatenate(
        [jnp.sum(x[4 * g : 4 * g + 4], axis=0, keepdims=True) for g in range(GROUPS)] + [pad],
        axis=0,
    )
    colv[...] = gather4(first).astype(I32)
    samp = gather4(second).astype(I32)
    keyv[...] = jnp.where(samp > 0, samp - 1 + ((iota((8, W), 1) >> 5) << 5), -1)

    @pl.loop(0, GROUPS)
    def _(g):
        key = keyv[pl.ds(g, 1), :]
        want = colv[pl.ds(g, 1), :]
        sums = onehot(iota((W, W), 0) == key)
        names = onehot(iota((cols, W), 0) == want)
        cmat[pl.ds(pl.multiple_of(g * W, W), W), :] = nt(sums, names).astype(BF16)

    b = iota((W, NBLK), 1)
    bs = (((b >> 3) & 1) * NZ) + (b >> 4)
    dlanes = onehot(iota((W, NBLK), 0) == 32 * ((bs + 2) & 3) + (b & 7))
    bs24 = bs[0:NS]
    target = jnp.sum(
        jnp.where(iota((NS, NBLK), 0) == bs24, nn(asked.astype(BF16), dlanes), 0.0),
        axis=0, keepdims=True,
    ).astype(I32)
    goes = jnp.where(iota((32, NBLK), 0) == target, 1.0, 0.0)
    earlier = onehot(iota((NBLK, NBLK), 0) < iota((NBLK, NBLK), 1))
    seat = nn(goes.astype(BF16), earlier) + (NB * iota((32, NBLK), 0)).astype(F32)
    seat = jnp.sum(goes * seat, axis=0, keepdims=True).astype(I32)
    perm = onehot(iota((NBLK, NBLK), 0) == seat)

    wait_bytes(hotbuf, hot_recv)
    hi, lo = split2(hotbuf[...])
    hl[0:hotc, 0:W] = hi
    hl[0:hotc, W : 2 * W] = lo
    half = NZ * SAMP
    for h in range(2):
        part = nn(cmat[half * h : half * (h + 1), :], hl[...])
        pbuf[h] = (part[:, :W] + part[:, W:]).reshape(NZ, SAMP, W)
    to_sib = pltpu.make_async_remote_copy(
        src_ref=pbuf.at[1 - core], dst_ref=sbuf, send_sem=sib_send, recv_sem=sib_recv,
        device_id={"shard": sib}, device_id_type=MESH,
    )
    to_sib.start()

    @pl.when(three)
    def _():
        wait_bytes(xbuf, one_recv)

    @pl.when(jnp.logical_not(three))
    def _():
        wait_bytes(xbuf.at[0:2], one_recv)

    def reorder(i):
        x = xbuf[i]
        hi = x.astype(BF16)
        rest = x - hi.astype(F32)
        mid = rest.astype(BF16)
        low = (rest - mid.astype(F32)).astype(BF16)
        y = nn(perm, jnp.concatenate([hi, mid, low], axis=1))
        ybuf[i] = (y[:, :W] + y[:, W : 2 * W]) + y[:, 2 * W :]

    reorder(0)
    reorder(1)

    @pl.when(three)
    def _():
        reorder(2)

    def deliver(peer, count, remote):
        src = ybuf.at[0:count, pl.ds(pl.multiple_of(peer * NB, NB), NB), :]
        dst = moved.at[pl.ds(first_row(me), count)]
        if remote:
            pltpu.make_async_remote_copy(
                src_ref=src, dst_ref=dst, send_sem=two_send, recv_sem=two_recv,
                device_id={"shard": peer}, device_id_type=MESH,
            ).start()
        else:
            pltpu.make_async_copy(src, dst, two_recv).start()

    def deliver_all(count):
        deliver(me, count, False)

        @pl.loop(1, NS)
        def _(k):
            deliver(lax.rem(me + k, NS), count, True)

    by_count(me, deliver_all)

    to_sib.wait_recv()
    pbuf[core] += sbuf[...]
    pltpu.make_async_copy(pbuf.at[core, chip], pin.at[chip], sum_recv).start()

    @pl.loop(1, NZ)
    def _(k):
        z = lax.rem(chip + k, NZ)
        pltpu.make_async_remote_copy(
            src_ref=pbuf.at[core, z], dst_ref=pin.at[chip],
            send_sem=sum_send, recv_sem=sum_recv,
            device_id={"shard": 2 * z + core}, device_id_type=MESH,
        ).start()

    wait_bytes(pin, sum_recv)
    total = pin[0]
    for z in range(1, NZ):
        total += pin[z]
    pooled[...] = total / lens.astype(F32)

    wait_bytes(moved, two_recv)
    to_sib.wait_send()
    wait_bytes(req.at[0 : NS - 1], req_send)
    wait_bytes(hotbuf.at[0 : hotc - HOTD], hot_send)
    wait_bytes(pin.at[0 : NZ - 1], sum_send)

    @pl.when(three)
    def _():
        wait_bytes(abuf.at[0 : BLK - 3], one_send)
        wait_bytes(xbuf.at[:, 0 : NBLK - NB, :], two_send)

    @pl.when(jnp.logical_not(three))
    def _():
        wait_bytes(abuf.at[0 : BLK - 2], one_send)
        wait_bytes(xbuf.at[0:2, 0 : NBLK - NB, :], two_send)


def local(table, hot_offsets, cold_dest, bag_ids, bag_len):
    ng = lax.axis_size("grp")
    hotc = ng * HOTD
    cols = hotc + ROWS
    dma = pltpu.SemaphoreType.DMA
    moved, pooled = pl.pallas_call(
        functools.partial(kernel, ng),
        out_shape=(
            jax.ShapeDtypeStruct((BLK, NB, W), F32),
            jax.ShapeDtypeStruct((SAMP, W), F32),
        ),
        in_specs=[pl.BlockSpec(memory_space=pl.ANY)] * 5,
        out_specs=(
            pl.BlockSpec(memory_space=pl.ANY),
            pl.BlockSpec(memory_space=pltpu.VMEM),
        ),
        scratch_shapes=[
            pltpu.VMEM((ROWS, W), F32),
            pltpu.VMEM((SAMP, BAG), I32),
            pltpu.SMEM((HOTD,), I32),
            pltpu.SMEM((NB,), I32),
            pltpu.SMEM((SAMP,), I32),
            pltpu.VMEM((BLK, NB, W), F32),
            pltpu.VMEM((cols, 2 * W), BF16),
            pltpu.VMEM((HOTD, W), F32),
            pltpu.VMEM((hotc, W), F32),
            pltpu.VMEM((NS, 1, W), F32),
            pltpu.VMEM((NS, 1, W), F32),
            pltpu.VMEM((3, NBLK, W), F32),
            pltpu.VMEM((3, NBLK, W), F32),
            pltpu.VMEM((NS * SAMP, cols), BF16),
            pltpu.VMEM((2, NZ, SAMP, W), F32),
            pltpu.VMEM((NZ, SAMP, W), F32),
            pltpu.VMEM((NZ, SAMP, W), F32),
            pltpu.VMEM((8, W), I32),
            pltpu.VMEM((8, W), I32),
            dma((5,)),
        ]
        + [dma(())] * 12,
        compiler_params=pltpu.CompilerParams(
            collective_id=0, has_side_effects=True, vmem_limit_bytes=24 * 1024 * 1024
        ),
    )(table, hot_offsets, cold_dest, bag_ids, bag_len)
    return moved.transpose(1, 0, 2).reshape(ROWS, W), pooled


def solution(mesh):
    return jax.shard_map(
        local,
        mesh=mesh,
        in_specs=(
            P(("grp", "shard"), None),
            P(("grp", "shard")),
            P(("grp", "shard")),
            P(("grp", "shard"), None),
            P(("grp", "shard")),
        ),
        out_specs=(P(("grp", "shard"), None), P(("grp", "shard"), None)),
        check_vma=False,
    )
```

time: 433 us -> 54.2 us (0.13)
  blocking collectives: 141 us -> 0 us
  waiting for transfers between devices: 90.7 us -> 0 us
  local copies, waits for them, and re-layouts: 89.5 us -> 3.1 us
  other arithmetic: 73.1 us -> 0 us
  Pallas kernels: 0 us -> 50.2 us
  starting transfers between devices: 16.9 us -> 0 us
  between operations: 15 us -> 0.68 us
  matrix products: 4.94 us -> 0 us
    reduce_scatter x1 -> x0, waiting for transfers between devices: 90.7 us -> none  [local(): lax.psum_scatter(lax.map(pool_block, col_blocks).reshape(count, width), '...]
    gather x7 -> x0, local copies, waits for them, and re-layouts: 81.6 us -> none  [the longest x1 76.2 us: local(): local_pos = inverse_pos[group_block]]
    unnamed x1 -> x0, blocking collectives: 77.9 us -> none
    while x12 -> x0, other arithmetic: 67 us -> none
    all_gather x2 -> x0, blocking collectives: 62.9 us -> none  [the longest x1 38 us: local(): hot_rows = lax.all_gather(hot_local, 'grp', axis=0, tiled=True)]
    pallas_call x0 -> x1, Pallas kernels: none -> 50.2 us  [local(): pl.pallas_call(functools.partial(kernel, ng), out_shape=(jax.ShapeDtypeSt...]
    all_to_all x1 -> x0, starting transfers between devices: 16.8 us -> none  [local(): lax.all_to_all(outgoing, 'shard', split_axis=0, concat_axis=0, tiled=True)]
    dot_general x3 -> x0, matrix products: 4.94 us -> none  [pool_block(): jnp.dot(counts, columns, precision=lax.Precision.HIGHEST, preferred_eleme...]
  transfers between devices with their start and end apart: 2 -> 0, of which waited for: 1 -> 0; matrix products, arithmetic and copies ran while one was open for 19% -> 0% of each run, Pallas kernels for 0% -> 0%
where the time goes in v1:
time: 54.2 us; the launch traced here: 54 us
  Pallas kernels  50.2 us (93%)
  local copies, waits for them, and re-layouts  3.1 us (6%)
  between operations  0.68 us (1%)
    pallas_call x1, Pallas kernels, local(): pl.pallas_call(functools.partial(kernel, ng), out_shape=(jax.ShapeDtypeSt...  50.2 us
    unnamed x10, local copies, waits for them, and re-layouts  2.35 us

profile of v1, /device:TPU:1, one launch (start us, length us, event | category | flops | bytes accessed | tf_op | source)
XLA Modules:
  0.0 54.0 jit_solution(4424097073008235944)
XLA Ops:
  0.6 0.0 copy-start.3
  0.6 0.0 copy-start.2
  0.7 0.0 copy-start.1
  0.7 0.8 %copy.8.ids_h = s32[32,16]{1,0:T(8,128)S(1)} copy(s32[32,16]{0,1:T(8,128)} %param.8) | data formatting | bytes 4096 | tf_op args[3]
  1.4 0.0 copy-done.3
  1.5 0.0 copy-done.2
  1.5 0.0 copy-done.1
  1.5 0.0 copy-start
  1.5 0.9 %copy-done = f32[512,128]{1,0:T(8,128)S(1)} copy-done((f32[512,128]{1,0:T(8,128)S(1)}, f32[512,128]{1,0:T(8,128)}, u32[]{:S(2)}) %copy-start) | copy-done | bytes 262168
  2.4 50.2 %shard_map.68 = (f32[64,8,128]{2,1,0:T(8,128)S(1)}, f32[32,128]{1,0:T(8,128)S(1)}) custom-call(f32[512,128]{1,0:T(8,128)S(1)} %copy-done, s32[16]{0:T(128)S(1)} %copy-done.1, s32[8]{0:T(128)S(1)} %copy-done.2, s32[32,16]{1,0:T(8,128)S(1)} %copy.8.ids_h, s32[32]{0:T(128)S(1)} %copy-done.3), custom_call_target="tpu_custom_call" | custom-call | tf_op jit(solution)/shard_map/pallas_call | solution.py:348
  52.6 0.8 %copy.9 = f32[8,64,128]{2,1,0:T(8,128)} copy(f32[8,64,128]{2,0,1:T(8,128)S(1)} %bitcast.2) | data formatting | bytes 524288 | tf_op jit(solution)/shard_map/transpose | solution.py:386
  53.4 0.6 %copy.11 = f32[32,128]{1,0:T(8,128)} copy(f32[32,128]{1,0:T(8,128)S(1)} %get-tuple-element.9) | data formatting | bytes 32768
Async XLA Ops:
  0.6 0.8 %copy-start.3 = (s32[32]{0:T(128)S(1)}, s32[32]{0:T(128)}, u32[]{:S(2)}) copy-start(s32[32]{0:T(128)} %len_h.1) | copy-start | bytes 388
  0.6 0.8 %copy-start.2 = (s32[8]{0:T(128)S(1)}, s32[8]{0:T(128)}, u32[]{:S(2)}) copy-start(s32[8]{0:T(128)} %dest_h.1) | copy-start | bytes 100
  0.7 0.8 %copy-start.1 = (s32[16]{0:T(128)S(1)}, s32[16]{0:T(128)}, u32[]{:S(2)}) copy-start(s32[16]{0:T(128)} %off_h.1) | copy-start | bytes 196
  1.5 1.0 %copy-start = (f32[512,128]{1,0:T(8,128)S(1)}, f32[512,128]{1,0:T(8,128)}, u32[]{:S(2)}) copy-start(f32[512,128]{1,0:T(8,128)} %table_h.1) | copy-start | bytes 786436

commit v2 on v1

v2 whole, which is shorter than its diff:
```python
import functools

import jax
import jax.numpy as jnp
from jax import lax
from jax.experimental import pallas as pl
from jax.experimental.pallas import tpu as pltpu
from jax.sharding import PartitionSpec as P

MESH = pl.DeviceIdType.MESH
F32 = jnp.float32
BF16 = jnp.bfloat16
I32 = jnp.int32

NS = 24
NZ = 12
HOP = 3
NB = 8
BLK = 64
W = 128
NBLK = NS * NB
SAMP = 32
BAG = 16
SLOTS = SAMP * BAG
HOTD = 16
ROWS = NB * BLK
GROUPS = NS // 4


def iota(shape, axis):
    return lax.broadcasted_iota(I32, shape, axis)


def onehot(mask):
    return jnp.where(mask, 1.0, 0.0).astype(BF16)


def nt(a, b):
    return lax.dot_general(a, b, (((1,), (1,)), ((), ())), preferred_element_type=F32)


def nn(a, b):
    return jnp.dot(a, b, preferred_element_type=F32)


def split2(x):
    hi = x.astype(BF16)
    return hi, (x - hi.astype(F32)).astype(BF16)


def first_row(m):
    return 8 * (m // 3) + 3 * lax.rem(m, 3)


def order(s):
    return lax.rem(s, 2) * NZ + s // 2


def far_first(me, n, act):
    act(lax.rem(me + n // 2, n))

    @pl.loop(1, n // 2)
    def _(q):
        act(lax.rem(me + n // 2 - q, n))
        act(lax.rem(me + n // 2 + q, n))


def wait_bytes(ref, sem):
    pltpu.make_async_copy(ref, ref, sem).wait()


def kernel(
    ng,
    table_h, off_h, dest_h, ids_h, len_h,
    moved, pooled,
    tbl, ids, off_s, dest_s, len_s,
    abuf, hl, hotloc, hotbuf, msg, req, xbuf, ybuf, cmat, pbuf, sbuf, rin, pin, colv, keyv,
    load_sem, req_send, req_recv, hot_send, hot_recv, one_send, one_recv, two_send, two_recv,
    sib_send, sib_recv, sum_send, sum_recv, far_recv,
):
    hotc = ng * HOTD
    cols = hotc + ROWS
    me = lax.axis_index("shard")
    grp = lax.axis_index("grp")
    core = lax.rem(me, 2)
    chip = me // 2
    sib = me + 1 - 2 * core
    mine = order(me)
    lane0 = lax.rem(mine, 4)
    three = lax.rem(me, 3) < 2

    loads = [
        pltpu.make_async_copy(table_h, tbl, load_sem.at[0]),
        pltpu.make_async_copy(ids_h, ids, load_sem.at[1]),
        pltpu.make_async_copy(len_h, len_s, load_sem.at[2]),
        pltpu.make_async_copy(off_h, off_s, load_sem.at[3]),
        pltpu.make_async_copy(dest_h, dest_s, load_sem.at[4]),
    ]
    for load in loads:
        load.start()

    barrier = pltpu.get_barrier_semaphore()

    def greet(where):
        pl.semaphore_signal(barrier, inc=1, device_id=where, device_id_type=MESH)

    far_first(me, NS, lambda peer: greet({"shard": peer}))
    far_first(grp, ng, lambda peer: greet({"grp": peer}))

    for load in loads[1:]:
        load.wait()

    lens = jnp.zeros((SAMP, W), I32)
    row = iota((SAMP, W), 0)
    for n in range(SAMP):
        lens = jnp.where(row == n, len_s[n], lens)
    bag = ids[...]
    hot_total = hotc * NS
    is_hot = bag < hot_total
    owner = bag >> 4
    turn = (owner * 43691) >> 20
    cold = jnp.maximum(bag - hot_total, 0)
    shard = jnp.where(is_hot, owner - turn * NS, cold >> 9)
    col = jnp.where(is_hot, turn * HOTD + (bag & (HOTD - 1)), hotc + (cold & (ROWS - 1)))
    square = iota((SAMP, SAMP), 0) == iota((SAMP, SAMP), 1)
    lens_row = jnp.sum(jnp.where(square, lens[:, :SAMP], 0), axis=0, keepdims=True)
    live = iota((BAG, SAMP), 0) < lens_row
    shard = jnp.where(live, shard, 31)
    fields = jnp.concatenate([shard, col >> 5, col & 31], axis=0).astype(F32).astype(BF16)
    spread = nn(fields, onehot(iota((SAMP, SLOTS), 0) == (iota((SAMP, SLOTS), 1) & (SAMP - 1))))
    own = iota((BAG, SLOTS), 0) == (iota((BAG, SLOTS), 1) >> 5)
    flat = [
        jnp.sum(jnp.where(own, spread[BAG * i : BAG * (i + 1)], 0.0), axis=0, keepdims=True)
        for i in range(3)
    ]
    to = jnp.where(flat[0] == iota((32, SLOTS), 0).astype(F32), 1.0, 0.0)
    to = jnp.where(iota((32, SLOTS), 0) < NS, to, 0.0)
    before = onehot(iota((SLOTS, SLOTS), 0) < iota((SLOTS, SLOTS), 1))
    rank = jnp.sum(to * nn(to.astype(BF16), before), axis=0, keepdims=True)
    place = onehot(
        rank.astype(I32) + 32 * lane0 == iota((W, SLOTS), 0)
    )
    sample1 = ((iota((1, SLOTS), 1) & (SAMP - 1)) + 1).astype(F32)
    packed = jnp.concatenate([to * flat[1], to * flat[2], to * sample1], axis=0).astype(BF16)
    placed = nt(packed, place)
    colpart = 32.0 * placed[0:NS] + placed[32 : 32 + NS]
    samppart = pltpu.roll(placed[64 : 64 + NS], 32, 1)
    dests = jnp.zeros((1, W), I32)
    lane = iota((1, W), 1)
    dlane = 32 * lax.rem(mine + 2, 4)
    for j in range(NB):
        dests = jnp.where(lane == dlane + j, dest_s[j], dests)
    msg[:, 0, :] = colpart + samppart + dests.astype(F32)

    loads[0].wait()
    hi, lo = split2(tbl[...])
    hl[hotc:cols, 0:W] = hi
    hl[hotc:cols, W : 2 * W] = lo
    offs = jnp.zeros((HOTD, ROWS), I32)
    hrow = iota((HOTD, ROWS), 0)
    for k in range(HOTD):
        offs = jnp.where(hrow == k, off_s[k], offs)
    picked = nn(onehot(offs == iota((HOTD, ROWS), 1)), hl[hotc:cols, :])
    hotloc[...] = picked[:, :W] + picked[:, W:]
    for r in range(BLK):
        abuf[r] = tbl[pl.ds(r, NB, stride=BLK), :]

    pl.semaphore_wait(barrier, NS - 1 + ng - 1)

    pltpu.make_async_copy(msg.at[pl.ds(me, 1)], req.at[pl.ds(mine, 1)], req_recv).start()

    far_first(me, NS, lambda peer: pltpu.make_async_remote_copy(
        src_ref=msg.at[pl.ds(peer, 1)], dst_ref=req.at[pl.ds(mine, 1)],
        send_sem=req_send, recv_sem=req_recv,
        device_id={"shard": peer}, device_id_type=MESH,
    ).start())

    hot_here = hotbuf.at[pl.ds(pl.multiple_of(grp * HOTD, HOTD), HOTD)]
    pltpu.make_async_copy(hotloc, hot_here, hot_recv).start()

    far_first(grp, ng, lambda peer: pltpu.make_async_remote_copy(
        src_ref=hotloc, dst_ref=hot_here, send_sem=hot_send, recv_sem=hot_recv,
        device_id={"grp": peer}, device_id_type=MESH,
    ).start())

    def push(src, dst, send_sem, recv_sem, peer):
        pltpu.make_async_remote_copy(
            src_ref=src, dst_ref=dst, send_sem=send_sem, recv_sem=recv_sem,
            device_id={"shard": peer}, device_id_type=MESH,
        ).start()

    def relay(peer, start, count):
        src = abuf.at[pl.ds(first_row(peer) + start, count)]
        dst = xbuf.at[
            start : start + count, pl.ds(pl.multiple_of(me * NB, NB), NB), :
        ]
        return src, dst

    def by_count(peer, act):
        @pl.when(lax.rem(peer, 3) < 2)
        def _():
            act(3)

        @pl.when(lax.rem(peer, 3) == 2)
        def _():
            act(2)

    pltpu.make_async_copy(*relay(me, 0, 1), one_recv.at[0]).start()
    by_count(
        me,
        lambda n: pltpu.make_async_copy(*relay(me, 1, n - 1), one_recv.at[1]).start(),
    )
    far_first(
        me, NS, lambda peer: push(*relay(peer, 0, 1), one_send, one_recv.at[0], peer)
    )
    far_first(me, NS, lambda peer: by_count(
        peer, lambda n: push(*relay(peer, 1, n - 1), one_send, one_recv.at[1], peer)
    ))

    wait_bytes(req, req_recv)
    asked = req[:, 0, :]
    b = iota((W, NBLK), 1)
    bs = (((b >> 3) & 1) * NZ) + (b >> 4)
    dlanes = onehot(iota((W, NBLK), 0) == 32 * ((bs + 2) & 3) + (b & 7))
    bs24 = bs[0:NS]
    target = jnp.sum(
        jnp.where(iota((NS, NBLK), 0) == bs24, nn(asked.astype(BF16), dlanes), 0.0),
        axis=0, keepdims=True,
    ).astype(I32)
    goes = jnp.where(iota((32, NBLK), 0) == target, 1.0, 0.0)
    earlier = onehot(iota((NBLK, NBLK), 0) < iota((NBLK, NBLK), 1))
    seat = nn(goes.astype(BF16), earlier) + (NB * iota((32, NBLK), 0)).astype(F32)
    seat = jnp.sum(goes * seat, axis=0, keepdims=True).astype(I32)
    perm = onehot(iota((NBLK, NBLK), 0) == seat)

    def reorder(i):
        x = xbuf[i]
        hi = x.astype(BF16)
        rest = x - hi.astype(F32)
        mid = rest.astype(BF16)
        low = (rest - mid.astype(F32)).astype(BF16)
        y = nn(perm, jnp.concatenate([hi, mid, low], axis=1))
        ybuf[i] = (y[:, :W] + y[:, W : 2 * W]) + y[:, 2 * W :]

    def deliver(peer, start, count):
        src = ybuf.at[
            start : start + count, pl.ds(pl.multiple_of(peer * NB, NB), NB), :
        ]
        return src, moved.at[pl.ds(first_row(me) + start, count)]

    def deliver_all(start, count):
        pltpu.make_async_copy(*deliver(me, start, count), two_recv).start()
        far_first(
            me, NS,
            lambda peer: push(*deliver(peer, start, count), two_send, two_recv, peer),
        )

    wait_bytes(xbuf.at[0:1], one_recv.at[0])
    reorder(0)
    deliver_all(0, 1)

    who = iota((NS, W), 0)
    spot = (iota((NS, W), 1) >> 5) & 3
    first = jnp.where(spot == (who & 3), asked, 0.0)
    second = pltpu.roll(jnp.where(spot == ((who + 1) & 3), asked, 0.0), W - 32, 1)
    pad = jnp.zeros((8 - GROUPS, W), F32)
    gather4 = lambda x: jnp.concatenate(
        [jnp.sum(x[4 * g : 4 * g + 4], axis=0, keepdims=True) for g in range(GROUPS)] + [pad],
        axis=0,
    )
    colv[...] = gather4(first).astype(I32)
    samp = gather4(second).astype(I32)
    keyv[...] = jnp.where(samp > 0, samp - 1 + ((iota((8, W), 1) >> 5) << 5), -1)

    @pl.loop(0, GROUPS)
    def _(g):
        key = keyv[pl.ds(g, 1), :]
        want = colv[pl.ds(g, 1), :]
        sums = onehot(iota((W, W), 0) == key)
        names = onehot(iota((cols, W), 0) == want)
        cmat[pl.ds(pl.multiple_of(g * W, W), W), :] = nt(sums, names).astype(BF16)

    wait_bytes(hotbuf, hot_recv)
    hi, lo = split2(hotbuf[...])
    hl[0:hotc, 0:W] = hi
    hl[0:hotc, W : 2 * W] = lo
    half = NZ * SAMP
    for h in range(2):
        part = nn(cmat[half * h : half * (h + 1), :], hl[...])
        pbuf[h] = (part[:, :W] + part[:, W:]).reshape(NZ, SAMP, W)
    to_sib = pltpu.make_async_remote_copy(
        src_ref=pbuf.at[1 - core], dst_ref=sbuf, send_sem=sib_send, recv_sem=sib_recv,
        device_id={"shard": sib}, device_id_type=MESH,
    )
    to_sib.start()
    to_sib.wait_recv()
    pbuf[core] += sbuf[...]
    pltpu.make_async_copy(pbuf.at[core, chip], pin.at[HOP], sum_recv).start()

    def chip_at(step):
        return lax.rem(chip + step + NZ, NZ)

    def send_sum(step, via, dst, recv_sem):
        push(
            pbuf.at[core, chip_at(step)], dst, sum_send, recv_sem,
            2 * chip_at(via) + core,
        )

    send_sum(6, 3 + 6 * core, rin.at[4], far_recv)
    for i, step in enumerate((-5, 5, -4, 4)):
        send_sum(step, step - HOP if step > 0 else step + HOP, rin.at[i], far_recv)
    for step in (-2, 2, -1, 1):
        send_sum(step, step, pin.at[HOP + step], sum_recv)

    by_count(me, lambda n: wait_bytes(xbuf.at[1:n], one_recv.at[1]))
    reorder(1)

    @pl.when(three)
    def _():
        reorder(2)

    by_count(me, lambda n: deliver_all(1, n - 1))

    wait_bytes(rin, far_recv)
    pbuf[core, chip_at(-HOP)] += rin[0] + rin[2]
    pbuf[core, chip_at(HOP)] += rin[1] + rin[3]
    pbuf[core, chip_at(HOP + 6 * core)] += rin[4]
    for step in (-HOP, HOP):
        send_sum(step, step, pin.at[HOP + step], sum_recv)
    wait_bytes(pin, sum_recv)
    total = pin[0]
    for z in range(1, 2 * HOP + 1):
        total += pin[z]
    pooled[...] = total / lens.astype(F32)

    wait_bytes(moved, two_recv)
    to_sib.wait_send()
    wait_bytes(req.at[0 : NS - 1], req_send)
    wait_bytes(hotbuf.at[0 : hotc - HOTD], hot_send)
    wait_bytes(pbuf.at[0, 0 : NZ - 1], sum_send)

    by_count(me, lambda n: wait_bytes(abuf.at[0 : BLK - n], one_send))
    by_count(me, lambda n: wait_bytes(xbuf.at[0:n, 0 : NBLK - NB, :], two_send))


def local(table, hot_offsets, cold_dest, bag_ids, bag_len):
    ng = lax.axis_size("grp")
    hotc = ng * HOTD
    cols = hotc + ROWS
    dma = pltpu.SemaphoreType.DMA
    moved, pooled = pl.pallas_call(
        functools.partial(kernel, ng),
        out_shape=(
            jax.ShapeDtypeStruct((BLK, NB, W), F32),
            jax.ShapeDtypeStruct((SAMP, W), F32),
        ),
        in_specs=[pl.BlockSpec(memory_space=pltpu.HBM)] * 5,
        out_specs=(
            pl.BlockSpec(memory_space=pl.ANY),
            pl.BlockSpec(memory_space=pltpu.VMEM),
        ),
        scratch_shapes=[
            pltpu.VMEM((ROWS, W), F32),
            pltpu.VMEM((BAG, SAMP), I32),
            pltpu.SMEM((HOTD,), I32),
            pltpu.SMEM((NB,), I32),
            pltpu.SMEM((SAMP,), I32),
            pltpu.VMEM((BLK, NB, W), F32),
            pltpu.VMEM((cols, 2 * W), BF16),
            pltpu.VMEM((HOTD, W), F32),
            pltpu.VMEM((hotc, W), F32),
            pltpu.VMEM((NS, 1, W), F32),
            pltpu.VMEM((NS, 1, W), F32),
            pltpu.VMEM((3, NBLK, W), F32),
            pltpu.VMEM((3, NBLK, W), F32),
            pltpu.VMEM((NS * SAMP, cols), BF16),
            pltpu.VMEM((2, NZ, SAMP, W), F32),
            pltpu.VMEM((NZ, SAMP, W), F32),
            pltpu.VMEM((5, SAMP, W), F32),
            pltpu.VMEM((2 * HOP + 1, SAMP, W), F32),
            pltpu.VMEM((8, W), I32),
            pltpu.VMEM((8, W), I32),
            dma((5,)),
        ]
        + [dma(())] * 5
        + [dma((2,))]
        + [dma(())] * 7,
        compiler_params=pltpu.CompilerParams(
            collective_id=0, has_side_effects=True, vmem_limit_bytes=24 * 1024 * 1024
        ),
    )(
        *(
            pltpu.with_memory_space_constraint(x, pltpu.HBM)
            for x in (table, hot_offsets, cold_dest, bag_ids.T, bag_len)
        )
    )
    return moved.transpose(1, 0, 2).reshape(ROWS, W), pooled


def solution(mesh):
    return jax.shard_map(
        local,
        mesh=mesh,
        in_specs=(
            P(("grp", "shard"), None),
            P(("grp", "shard")),
            P(("grp", "shard")),
            P(("grp", "shard"), None),
            P(("grp", "shard")),
        ),
        out_specs=(P(("grp", "shard"), None), P(("grp", "shard"), None)),
        check_vma=False,
    )
```

time: 54.2 us -> 46.4 us (0.86)
  Pallas kernels: 50.2 us -> 44.3 us
  local copies, waits for them, and re-layouts: 3.1 us -> 1.36 us
    pallas_call x1, Pallas kernels: 50.2 us -> 44.3 us  [local(): pl.pallas_call(functools.partial(kernel, ng), out_shape=(jax.ShapeDtypeSt...]
    unnamed x10 -> x1, local copies, waits for them, and re-layouts: 2.35 us -> 0.6 us
where the time goes in v2:
time: 46.4 us; the launch traced here: 46.3 us
  Pallas kernels  44.3 us (95%)
  local copies, waits for them, and re-layouts  1.36 us (3%)
  between operations  0.64 us (1%)
    pallas_call x1, Pallas kernels, local(): pl.pallas_call(functools.partial(kernel, ng), out_shape=(jax.ShapeDtypeSt...  44.3 us

profile of v2, /device:TPU:1, one launch (start us, length us, event | category | flops | bytes accessed | tf_op | source)
XLA Modules:
  0.0 46.3 jit_solution(3070008992568380103)
XLA Ops:
  0.6 44.3 %shard_map.68 = (f32[64,8,128]{2,1,0:T(8,128)S(1)}, f32[32,128]{1,0:T(8,128)S(1)}) custom-call(f32[512,128]{1,0:T(8,128)} %table_h.1, s32[16]{0:T(128)} %off_h.1, s32[8]{0:T(128)} %dest_h.1, s32[16,32]{1,0:T(8,128)} %bitcast.5, s32[32]{0:T(128)} %len_h.1), custom_call_target="tpu_custom_call" | custom-call | tf_op jit(solution)/shard_map/pallas_call | solution.py:351
  44.9 0.8 %copy.7 = f32[8,64,128]{2,1,0:T(8,128)} copy(f32[8,64,128]{2,0,1:T(8,128)S(1)} %bitcast.3) | data formatting | bytes 524288 | tf_op jit(solution)/shard_map/transpose | solution.py:397
  45.7 0.6 %copy.9 = f32[32,128]{1,0:T(8,128)} copy(f32[32,128]{1,0:T(8,128)S(1)} %get-tuple-element.9) | data formatting | bytes 32768

commit v3 on v2

--- a/solution.py
+++ b/solution.py
@@ -77,6 +77,7 @@
     abuf, hl, hotloc, hotbuf, msg, req, xbuf, ybuf, cmat, pbuf, sbuf, rin, pin, colv, keyv,
     load_sem, req_send, req_recv, hot_send, hot_recv, one_send, one_recv, two_send, two_recv,
     sib_send, sib_recv, sum_send, sum_recv, far_recv,
+    column_sem, plane_sem,
 ):
     hotc = ng * HOTD
     cols = hotc + ROWS
@@ -89,6 +90,15 @@
     lane0 = lax.rem(mine, 4)
     three = lax.rem(me, 3) < 2
 
+    barrier = pltpu.get_barrier_semaphore()
+
+    def greet(where):
+        pl.semaphore_signal(barrier, inc=1, device_id=where, device_id_type=MESH)
+
+    far_first(chip, NZ, lambda z: greet({"shard": 2 * z}))
+    far_first(grp, ng, lambda g: greet({"grp": g, "shard": 2 * chip + 1}))
+    greet({"shard": sib})
+
     loads = [
         pltpu.make_async_copy(table_h, tbl, load_sem.at[0]),
         pltpu.make_async_copy(ids_h, ids, load_sem.at[1]),
@@ -98,14 +108,6 @@
     ]
     for load in loads:
         load.start()
-
-    barrier = pltpu.get_barrier_semaphore()
-
-    def greet(where):
-        pl.semaphore_signal(barrier, inc=1, device_id=where, device_id_type=MESH)
-
-    far_first(me, NS, lambda peer: greet({"shard": peer}))
-    far_first(grp, ng, lambda peer: greet({"grp": peer}))
 
     for load in loads[1:]:
         load.wait()
@@ -165,7 +167,17 @@
     for r in range(BLK):
         abuf[r] = tbl[pl.ds(r, NB, stride=BLK), :]
 
-    pl.semaphore_wait(barrier, NS - 1 + ng - 1)
+    def tell(sem):
+        pl.semaphore_signal(sem, inc=1, device_id={"shard": sib}, device_id_type=MESH)
+
+    @pl.when(core == 0)
+    def _():
+        pl.semaphore_wait(barrier, NS - 1)
+        tell(column_sem)
+
+    @pl.when(core == 1)
+    def _():
+        pl.semaphore_wait(column_sem, 1)
 
     pltpu.make_async_copy(msg.at[pl.ds(me, 1)], req.at[pl.ds(mine, 1)], req_recv).start()
 
@@ -173,14 +185,6 @@
         src_ref=msg.at[pl.ds(peer, 1)], dst_ref=req.at[pl.ds(mine, 1)],
         send_sem=req_send, recv_sem=req_recv,
         device_id={"shard": peer}, device_id_type=MESH,
-    ).start())
-
-    hot_here = hotbuf.at[pl.ds(pl.multiple_of(grp * HOTD, HOTD), HOTD)]
-    pltpu.make_async_copy(hotloc, hot_here, hot_recv).start()
-
-    far_first(grp, ng, lambda peer: pltpu.make_async_remote_copy(
-        src_ref=hotloc, dst_ref=hot_here, send_sem=hot_send, recv_sem=hot_recv,
-        device_id={"grp": peer}, device_id_type=MESH,
     ).start())
 
     def push(src, dst, send_sem, recv_sem, peer):
@@ -216,6 +220,23 @@
     far_first(me, NS, lambda peer: by_count(
         peer, lambda n: push(*relay(peer, 1, n - 1), one_send, one_recv.at[1], peer)
     ))
+
+    @pl.when(core == 1)
+    def _():
+        pl.semaphore_wait(barrier, 2 * ng - 1)
+        tell(plane_sem)
+
+    @pl.when(core == 0)
+    def _():
+        pl.semaphore_wait(plane_sem, 1)
+
+    hot_here = hotbuf.at[pl.ds(pl.multiple_of(grp * HOTD, HOTD), HOTD)]
+    pltpu.make_async_copy(hotloc, hot_here, hot_recv).start()
+
+    far_first(grp, ng, lambda peer: pltpu.make_async_remote_copy(
+        src_ref=hotloc, dst_ref=hot_here, send_sem=hot_send, recv_sem=hot_recv,
+        device_id={"grp": peer}, device_id_type=MESH,
+    ).start())
 
     wait_bytes(req, req_recv)
     asked = req[:, 0, :]
@@ -255,10 +276,6 @@
             lambda peer: push(*deliver(peer, start, count), two_send, two_recv, peer),
         )
 
-    wait_bytes(xbuf.at[0:1], one_recv.at[0])
-    reorder(0)
-    deliver_all(0, 1)
-
     who = iota((NS, W), 0)
     spot = (iota((NS, W), 1) >> 5) & 3
     first = jnp.where(spot == (who & 3), asked, 0.0)
@@ -279,6 +296,10 @@
         sums = onehot(iota((W, W), 0) == key)
         names = onehot(iota((cols, W), 0) == want)
         cmat[pl.ds(pl.multiple_of(g * W, W), W), :] = nt(sums, names).astype(BF16)
+
+    wait_bytes(xbuf.at[0:1], one_recv.at[0])
+    reorder(0)
+    deliver_all(0, 1)
 
     wait_bytes(hotbuf, hot_recv)
     hi, lo = split2(hotbuf[...])
@@ -341,6 +362,12 @@
 
     by_count(me, lambda n: wait_bytes(abuf.at[0 : BLK - n], one_send))
     by_count(me, lambda n: wait_bytes(xbuf.at[0:n, 0 : NBLK - NB, :], two_send))
+
+
+def finish(moved, sums, table, pooled):
+    for r in range(BLK):
+        table[pl.ds(r, NB, stride=BLK), :] = moved[r]
+    pooled[...] = sums[...]
 
 
 def local(table, hot_offsets, cold_dest, bag_ids, bag_len):
@@ -384,7 +411,8 @@
         ]
         + [dma(())] * 5
         + [dma((2,))]
-        + [dma(())] * 7,
+        + [dma(())] * 7
+        + [pltpu.SemaphoreType.REGULAR] * 2,
         compiler_params=pltpu.CompilerParams(
             collective_id=0, has_side_effects=True, vmem_limit_bytes=24 * 1024 * 1024
         ),
@@ -394,7 +422,18 @@
             for x in (table, hot_offsets, cold_dest, bag_ids.T, bag_len)
         )
     )
-    return moved.transpose(1, 0, 2).reshape(ROWS, W), pooled
+    return pl.pallas_call(
+        finish,
+        out_shape=(
+            jax.ShapeDtypeStruct((ROWS, W), F32),
+            jax.ShapeDtypeStruct((SAMP, W), F32),
+        ),
+        in_specs=[pl.BlockSpec(memory_space=pltpu.VMEM)] * 2,
+        out_specs=[pl.BlockSpec(memory_space=pltpu.VMEM)] * 2,
+    )(
+        pltpu.with_memory_space_constraint(moved, pltpu.VMEM),
+        pltpu.with_memory_space_constraint(pooled, pltpu.VMEM),
+    )
 
 
 def solution(mesh):

time: 46.4 us -> 45.1 us (0.972)
  local copies, waits for them, and re-layouts: 1.36 us -> 0 us
    pallas_call x0 -> x1, Pallas kernels: none -> 0.85 us  [local(): pl.pallas_call(finish, out_shape=(jax.ShapeDtypeStruct((ROWS, W), F32), j...]
    pallas_call x1, Pallas kernels: 44.3 us -> 43.5 us  [local(): pl.pallas_call(functools.partial(kernel, ng), out_shape=(jax.ShapeDtypeSt...]
    transpose x1 -> x0, local copies, waits for them, and re-layouts: 0.75 us -> none  [local(): return (moved.transpose(1, 0, 2).reshape(ROWS, W), pooled)]
    unnamed x1 -> x0, local copies, waits for them, and re-layouts: 0.6 us -> none
where the time goes in v3:
time: 45.1 us; the launch traced here: 45 us
  Pallas kernels  44.4 us (98%)
  between operations  0.64 us (1%)
    pallas_call x1, Pallas kernels, local(): pl.pallas_call(functools.partial(kernel, ng), out_shape=(jax.ShapeDtypeSt...  43.5 us

profile of v3, /device:TPU:1, one launch (start us, length us, event | category | flops | bytes accessed | tf_op | source)
XLA Modules:
  0.0 45.0 jit_solution(16972698108142340785)
XLA Ops:
  0.6 43.5 %shard_map.68 = (f32[64,8,128]{2,1,0:T(8,128)S(1)}, f32[32,128]{1,0:T(8,128)S(1)}) custom-call(f32[512,128]{1,0:T(8,128)} %table_h.1, s32[16]{0:T(128)} %off_h.1, s32[8]{0:T(128)} %dest_h.1, s32[16,32]{1,0:T(8,128)} %bitcast.1, s32[32]{0:T(128)} %len_h.1), custom_call_target="tpu_custom_call" | custom-call | tf_op jit(solution)/shard_map/pallas_call | solution.py:378
  44.1 0.9 %shard_map.69 = (f32[512,128]{1,0:T(8,128)}, f32[32,128]{1,0:T(8,128)}) custom-call(f32[64,8,128]{2,1,0:T(8,128)S(1)} %get-tuple-element.4.moved, f32[32,128]{1,0:T(8,128)S(1)} %get-tuple-element.5.sums), custom_call_target="tpu_custom_call" | custom-call | tf_op jit(solution)/shard_map/pallas_call | solution.py:425

commit v4 on v3

--- a/solution.py
+++ b/solution.py
@@ -210,16 +210,25 @@
             act(2)
 
     pltpu.make_async_copy(*relay(me, 0, 1), one_recv.at[0]).start()
-    by_count(
-        me,
-        lambda n: pltpu.make_async_copy(*relay(me, 1, n - 1), one_recv.at[1]).start(),
-    )
+    pltpu.make_async_copy(*relay(me, 1, 1), one_recv.at[1]).start()
+
+    @pl.when(three)
+    def _():
+        pltpu.make_async_copy(*relay(me, 2, 1), one_recv.at[2]).start()
+
     far_first(
         me, NS, lambda peer: push(*relay(peer, 0, 1), one_send, one_recv.at[0], peer)
     )
-    far_first(me, NS, lambda peer: by_count(
-        peer, lambda n: push(*relay(peer, 1, n - 1), one_send, one_recv.at[1], peer)
-    ))
+    far_first(
+        me, NS, lambda peer: push(*relay(peer, 1, 1), one_send, one_recv.at[1], peer)
+    )
+
+    def third(peer):
+        @pl.when(lax.rem(peer, 3) < 2)
+        def _():
+            push(*relay(peer, 2, 1), one_send, one_recv.at[2], peer)
+
+    far_first(me, NS, third)
 
     @pl.when(core == 1)
     def _():
@@ -301,6 +310,10 @@
     reorder(0)
     deliver_all(0, 1)
 
+    wait_bytes(xbuf.at[1:2], one_recv.at[1])
+    reorder(1)
+    deliver_all(1, 1)
+
     wait_bytes(hotbuf, hot_recv)
     hi, lo = split2(hotbuf[...])
     hl[0:hotc, 0:W] = hi
@@ -333,14 +346,12 @@
     for step in (-2, 2, -1, 1):
         send_sum(step, step, pin.at[HOP + step], sum_recv)
 
-    by_count(me, lambda n: wait_bytes(xbuf.at[1:n], one_recv.at[1]))
-    reorder(1)
 
     @pl.when(three)
     def _():
+        wait_bytes(xbuf.at[2:3], one_recv.at[2])
         reorder(2)
-
-    by_count(me, lambda n: deliver_all(1, n - 1))
+        deliver_all(2, 1)
 
     wait_bytes(rin, far_recv)
     pbuf[core, chip_at(-HOP)] += rin[0] + rin[2]
@@ -410,7 +421,7 @@
             dma((5,)),
         ]
         + [dma(())] * 5
-        + [dma((2,))]
+        + [dma((3,))]
         + [dma(())] * 7
         + [pltpu.SemaphoreType.REGULAR] * 2,
         compiler_params=pltpu.CompilerParams(

time: 45.1 us -> 43.7 us (0.969)
  Pallas kernels: 44.4 us -> 42.9 us
    pallas_call x1, Pallas kernels: 43.5 us -> 42 us  [local(): pl.pallas_call(functools.partial(kernel, ng), out_shape=(jax.ShapeDtypeSt...]
where the time goes in v4:
time: 43.7 us; the launch traced here: 43.5 us
  Pallas kernels  42.9 us (98%)
  between operations  0.64 us (1%)
    pallas_call x1, Pallas kernels, local(): pl.pallas_call(functools.partial(kernel, ng), out_shape=(jax.ShapeDtypeSt...  42 us

profile of v4, /device:TPU:1, one launch (start us, length us, event | category | flops | bytes accessed | tf_op | source)
XLA Modules:
  0.0 43.5 jit_solution(3428096009363148485)
XLA Ops:
  0.6 42.0 %shard_map.68 = (f32[64,8,128]{2,1,0:T(8,128)S(1)}, f32[32,128]{1,0:T(8,128)S(1)}) custom-call(f32[512,128]{1,0:T(8,128)} %table_h.1, s32[16]{0:T(128)} %off_h.1, s32[8]{0:T(128)} %dest_h.1, s32[16,32]{1,0:T(8,128)} %bitcast.1, s32[32]{0:T(128)} %len_h.1), custom_call_target="tpu_custom_call" | custom-call | tf_op jit(solution)/shard_map/pallas_call | solution.py:389
  42.7 0.9 %shard_map.69 = (f32[512,128]{1,0:T(8,128)}, f32[32,128]{1,0:T(8,128)}) custom-call(f32[64,8,128]{2,1,0:T(8,128)S(1)} %get-tuple-element.4.moved, f32[32,128]{1,0:T(8,128)S(1)} %get-tuple-element.5.sums), custom_call_target="tpu_custom_call" | custom-call | tf_op jit(solution)/shard_map/pallas_call | solution.py:436

commit v5 on v4

--- a/solution.py
+++ b/solution.py
@@ -63,6 +63,15 @@
     def _(q):
         act(lax.rem(me + n // 2 - q, n))
         act(lax.rem(me + n // 2 + q, n))
+
+
+def far_first_plane(me, n, act):
+    nx, ny = (4, 8) if n == 32 else (1, n)
+    x, y = me // ny, lax.rem(me, ny)
+    steps = [(i, j) for i in range(nx) for j in range(ny) if i or j]
+    steps.sort(key=lambda p: min(p[0], nx - p[0]) + min(p[1], ny - p[1]), reverse=True)
+    for i, j in steps:
+        act(lax.rem(x + i, nx) * ny + lax.rem(y + j, ny))
 
 
 def wait_bytes(ref, sem):
@@ -96,7 +105,7 @@
         pl.semaphore_signal(barrier, inc=1, device_id=where, device_id_type=MESH)
 
     far_first(chip, NZ, lambda z: greet({"shard": 2 * z}))
-    far_first(grp, ng, lambda g: greet({"grp": g, "shard": 2 * chip + 1}))
+    far_first_plane(grp, ng, lambda g: greet({"grp": g, "shard": 2 * chip + 1}))
     greet({"shard": sib})
 
     loads = [
@@ -242,7 +251,7 @@
     hot_here = hotbuf.at[pl.ds(pl.multiple_of(grp * HOTD, HOTD), HOTD)]
     pltpu.make_async_copy(hotloc, hot_here, hot_recv).start()
 
-    far_first(grp, ng, lambda peer: pltpu.make_async_remote_copy(
+    far_first_plane(grp, ng, lambda peer: pltpu.make_async_remote_copy(
         src_ref=hotloc, dst_ref=hot_here, send_sem=hot_send, recv_sem=hot_recv,
         device_id={"grp": peer}, device_id_type=MESH,
     ).start())

time: 43.7 us -> 42.6 us (0.975)
  Pallas kernels: 42.9 us -> 41.8 us
    pallas_call x1, Pallas kernels: 42 us -> 40.9 us  [local(): pl.pallas_call(functools.partial(kernel, ng), out_shape=(jax.ShapeDtypeSt...]
where the time goes in v5:
time: 42.6 us; the launch traced here: 42.4 us
  Pallas kernels  41.8 us (98%)
  between operations  0.64 us (2%)
    pallas_call x1, Pallas kernels, local(): pl.pallas_call(functools.partial(kernel, ng), out_shape=(jax.ShapeDtypeSt...  40.9 us
    pallas_call x1, Pallas kernels, local(): pl.pallas_call(finish, out_shape=(jax.ShapeDtypeStruct((ROWS, W), F32), j...  0.85 us

profile of v5, /device:TPU:1, one launch (start us, length us, event | category | flops | bytes accessed | tf_op | source)
XLA Modules:
  0.0 42.4 jit_solution(7435461888329914946)
XLA Ops:
  0.6 40.9 %shard_map.68 = (f32[64,8,128]{2,1,0:T(8,128)S(1)}, f32[32,128]{1,0:T(8,128)S(1)}) custom-call(f32[512,128]{1,0:T(8,128)} %table_h.1, s32[16]{0:T(128)} %off_h.1, s32[8]{0:T(128)} %dest_h.1, s32[16,32]{1,0:T(8,128)} %bitcast.1, s32[32]{0:T(128)} %len_h.1), custom_call_target="tpu_custom_call" | custom-call | tf_op jit(solution)/shard_map/pallas_call | solution.py:398
  41.6 0.9 %shard_map.69 = (f32[512,128]{1,0:T(8,128)}, f32[32,128]{1,0:T(8,128)}) custom-call(f32[64,8,128]{2,1,0:T(8,128)S(1)} %get-tuple-element.4.moved, f32[32,128]{1,0:T(8,128)S(1)} %get-tuple-element.5.sums), custom_call_target="tpu_custom_call" | custom-call | tf_op jit(solution)/shard_map/pallas_call | solution.py:445

commit v6 on v5

--- a/solution.py
+++ b/solution.py
@@ -294,6 +294,10 @@
             lambda peer: push(*deliver(peer, start, count), two_send, two_recv, peer),
         )
 
+    wait_bytes(xbuf.at[0:1], one_recv.at[0])
+    reorder(0)
+    deliver_all(0, 1)
+
     who = iota((NS, W), 0)
     spot = (iota((NS, W), 1) >> 5) & 3
     first = jnp.where(spot == (who & 3), asked, 0.0)
@@ -315,9 +319,6 @@
         names = onehot(iota((cols, W), 0) == want)
         cmat[pl.ds(pl.multiple_of(g * W, W), W), :] = nt(sums, names).astype(BF16)
 
-    wait_bytes(xbuf.at[0:1], one_recv.at[0])
-    reorder(0)
-    deliver_all(0, 1)
 
     wait_bytes(xbuf.at[1:2], one_recv.at[1])
     reorder(1)
@@ -352,8 +353,6 @@
     send_sum(6, 3 + 6 * core, rin.at[4], far_recv)
     for i, step in enumerate((-5, 5, -4, 4)):
         send_sum(step, step - HOP if step > 0 else step + HOP, rin.at[i], far_recv)
-    for step in (-2, 2, -1, 1):
-        send_sum(step, step, pin.at[HOP + step], sum_recv)
 
 
     @pl.when(three)
@@ -361,6 +360,9 @@
         wait_bytes(xbuf.at[2:3], one_recv.at[2])
         reorder(2)
         deliver_all(2, 1)
+
+    for step in (-2, 2, -1, 1):
+        send_sum(step, step, pin.at[HOP + step], sum_recv)
 
     wait_bytes(rin, far_recv)
     pbuf[core, chip_at(-HOP)] += rin[0] + rin[2]
@@ -384,10 +386,15 @@
     by_count(me, lambda n: wait_bytes(xbuf.at[0:n, 0 : NBLK - NB, :], two_send))
 
 
-def finish(moved, sums, table, pooled):
-    for r in range(BLK):
-        table[pl.ds(r, NB, stride=BLK), :] = moved[r]
-    pooled[...] = sums[...]
+def finish(moved, sums, table, pooled, rows, sem):
+    small = pltpu.make_async_copy(sums, pooled, sem.at[1])
+    small.start()
+    for k in range(NB):
+        block = pl.ds(k * BLK, BLK)
+        rows[block, :] = moved[:, k, :]
+        pltpu.make_async_copy(rows.at[block], table.at[block], sem.at[0]).start()
+    wait_bytes(rows, sem.at[0])
+    small.wait()
 
 
 def local(table, hot_offsets, cold_dest, bag_ids, bag_len):
@@ -449,7 +456,8 @@
             jax.ShapeDtypeStruct((SAMP, W), F32),
         ),
         in_specs=[pl.BlockSpec(memory_space=pltpu.VMEM)] * 2,
-        out_specs=[pl.BlockSpec(memory_space=pltpu.VMEM)] * 2,
+        out_specs=[pl.BlockSpec(memory_space=pltpu.HBM)] * 2,
+        scratch_shapes=[pltpu.VMEM((ROWS, W), F32), pltpu.SemaphoreType.DMA((2,))],
     )(
         pltpu.with_memory_space_constraint(moved, pltpu.VMEM),
         pltpu.with_memory_space_constraint(pooled, pltpu.VMEM),

time: 42.6 us -> 42.2 us (level)
  no operation moved by 1% of the time
where the time goes in v6:
time: 42.2 us; the launch traced here: 42 us
  Pallas kernels  41.4 us (98%)
  between operations  0.64 us (2%)
    pallas_call x1, Pallas kernels, local(): pl.pallas_call(functools.partial(kernel, ng), out_shape=(jax.ShapeDtypeSt...  40.6 us

profile of v6, /device:TPU:1, one launch (start us, length us, event | category | flops | bytes accessed | tf_op | source)
XLA Modules:
  0.0 42.0 jit_solution(15498985140064302257)
XLA Ops:
  0.6 40.6 %shard_map.68 = (f32[64,8,128]{2,1,0:T(8,128)S(1)}, f32[32,128]{1,0:T(8,128)S(1)}) custom-call(f32[512,128]{1,0:T(8,128)} %table_h.1, s32[16]{0:T(128)} %off_h.1, s32[8]{0:T(128)} %dest_h.1, s32[16,32]{1,0:T(8,128)} %bitcast.1, s32[32]{0:T(128)} %len_h.1), custom_call_target="tpu_custom_call" | custom-call | tf_op jit(solution)/shard_map/pallas_call | solution.py:405
  41.2 0.8 %shard_map.69 = (f32[512,128]{1,0:T(8,128)}, f32[32,128]{1,0:T(8,128)}) custom-call(f32[64,8,128]{2,1,0:T(8,128)S(1)} %get-tuple-element.4.moved, f32[32,128]{1,0:T(8,128)S(1)} %get-tuple-element.5.sums), custom_call_target="tpu_custom_call" | custom-call | tf_op jit(solution)/shard_map/pallas_call | solution.py:452
